TPU v7x, 256 devices: a whole 4x4x8 slice. The times are simulated.
256 devices in a mesh: blk: 64 (over y, z_hi, x, core), head: 4 (over z_lo).
Axes of the slice: x: 4, y: 4, z: 8 (z_hi: 2, z_lo: 4; z = z_hi * 4 + z_lo), core: 2. Of those that a mesh axis runs over, the one named last changes fastest.
Arguments:
- query_in: bfloat16 [8192, 2048], P(('blk', 'head')), may hold values from -6 to 6
- key_in: bfloat16 [8192, 2048], P(('blk', 'head')), may hold values from -6 to 6
- value_in: bfloat16 [8192, 2048], P(('blk', 'head')), may hold values from -6 to 6
- saved_out: bfloat16 [8192, 2048], P(('blk', 'head')), may hold values from -0.59765625 to 0.59765625
- grad_out: bfloat16 [8192, 2048], P(('blk', 'head')), may hold values from -6 to 6
- saved_lse: float32 [8192, 16], P('blk', 'head'), may hold values from 3 to 6
- row_block: int32 [8192], replicated, may hold values from 0 to 15, as said below
- row_copy: int32 [8192], replicated, may hold values from 0 to 1, as said below
Outputs:
- grad_query: bfloat16 [8192, 2048], P(('blk', 'head'))
- grad_key: bfloat16 [8192, 2048], P(('blk', 'head'))
- grad_value: bfloat16 [8192, 2048], P(('blk', 'head'))
Inputs may be any that keep to these rules, and one draw needn't show every extreme that they name: `row_block`: rows g * 2 * 256 to (g + 1) * 2 * 256 - 1 all carry one block id, and each of the 16 ids is carried by exactly one such run. `row_copy`: in each aligned run of 128 rows exactly 64 rows are 1.
All inputs are finite; a program needn't handle non-finite values.
Results may differ from a plain program's by a relative error of at most 0.0085.
Values may be sent and summed in bfloat16 or wider, within the bound.
No kernel may reach another device: no remote copies, remote signals or barrier semaphores. Data moves between devices by JAX's collectives and lax.ppermute only.
A program may use at most 192 MiB of HBM per device.

v0:
```python
from functools import partial

import jax
import jax.numpy as jnp
from jax import lax
from jax.sharding import PartitionSpec as P

HD = 128
BLOCK = 256


def shifted(block, axis, distance):
    devices = range(lax.axis_size(axis))
    route = [(i - distance, i) for i in devices if i - distance in devices]
    return lax.ppermute(block, axis, route)


def tile_grads(
    queries, grad_rows, row_lse, row_delta, key_rows, value_rows, allowed, want_query, want_keys
):
    scaling = queries.shape[-1] ** (-0.5)
    scores = (
        jnp.einsum("qhd,khd->hqk", queries, key_rows, preferred_element_type=jnp.float32) * scaling
    )
    weights = jnp.where(allowed[None], jnp.exp(scores - jnp.transpose(row_lse)[:, :, None]), 0.0)
    dweights = jnp.einsum("qhd,khd->hqk", grad_rows, value_rows, preferred_element_type=jnp.float32)
    dscores = (weights * (dweights - jnp.transpose(row_delta)[:, :, None])).astype(jnp.bfloat16)
    results = []
    if want_query:
        results.append(
            scaling
            * jnp.einsum("hqk,khd->qhd", dscores, key_rows, preferred_element_type=jnp.float32)
        )
    if want_keys:
        results.append(
            scaling
            * jnp.einsum("hqk,qhd->khd", dscores, queries, preferred_element_type=jnp.float32)
        )
        results.append(
            jnp.einsum(
                "hqk,qhd->khd",
                weights.astype(jnp.bfloat16),
                grad_rows,
                preferred_element_type=jnp.float32,
            )
        )
    return tuple(results)


def per_device(query_in, key_in, value_in, saved_out, grad_out, saved_lse, row_block, row_copy):
    cycle_size = lax.axis_size("blk")
    my_index = lax.axis_index("blk")
    local_heads = saved_lse.shape[1]
    queries, key_rows, value_rows, outputs, grad_rows = (
        lax.all_to_all(query_in, "head", split_axis=1, concat_axis=0, tiled=True),
        lax.all_to_all(key_in, "head", split_axis=1, concat_axis=0, tiled=True),
        lax.all_to_all(value_in, "head", split_axis=1, concat_axis=0, tiled=True),
        lax.all_to_all(saved_out, "head", split_axis=1, concat_axis=0, tiled=True),
        lax.all_to_all(grad_out, "head", split_axis=1, concat_axis=0, tiled=True),
    )
    shard_rows = queries.shape[0]
    half_rows = shard_rows // 2
    head_shape = (shard_rows, local_heads, HD)
    queries = queries.reshape(head_shape)
    key_rows = key_rows.reshape(head_shape)
    value_rows = value_rows.reshape(head_shape)
    grad_rows = grad_rows.reshape(head_shape)
    row_delta = jnp.sum(
        grad_rows.astype(jnp.float32) * outputs.reshape(head_shape).astype(jnp.float32), axis=2
    )
    shard_block = row_block.reshape(cycle_size, shard_rows)[:, 0]
    own_block = shard_block[my_index]
    own_copy = lax.dynamic_slice_in_dim(row_copy, my_index * shard_rows, shard_rows)
    row_order = jnp.argsort(own_copy, stable=True)
    noisy_rows = row_order[:half_rows]
    clean_rows = row_order[half_rows:]
    clean_keys = key_rows[clean_rows]
    clean_values = value_rows[clean_rows]
    clean_blocks = jnp.repeat(shard_block, half_rows, total_repeat_length=cycle_size * half_rows)
    zero_query = jnp.zeros(head_shape, jnp.float32)
    initial = (zero_query,)
    totals = initial
    key_piece = lax.all_gather(clean_keys, "blk", axis=0, tiled=True)
    value_piece = lax.all_gather(clean_values, "blk", axis=0, tiled=True)
    piece_rows = key_piece.shape[0]
    blocks = lax.slice_in_dim(clean_blocks, 0, piece_rows, axis=0)
    totals = list(totals)
    for offset_rows in range(0, piece_rows, 512):
        span_rows = min(512, piece_rows - offset_rows)
        span_blocks = blocks[offset_rows : offset_rows + span_rows]
        add_allowed = (span_blocks[None, :] < own_block) | (span_blocks[None, :] == own_block) & (
            own_copy[:, None] == 1
        )
        add_compute = partial(
            tile_grads,
            queries,
            grad_rows,
            saved_lse,
            row_delta,
            key_piece[offset_rows : offset_rows + span_rows],
            value_piece[offset_rows : offset_rows + span_rows],
            add_allowed,
            True,
            False,
        )
        add_results = add_compute()
        totals[0] = totals[0] + add_results[0]
    folded = tuple(totals)
    grad_query = folded[0]
    clean_shape = (half_rows, local_heads, HD)
    every_lse, every_delta = (
        lax.all_gather(saved_lse, "blk", axis=0, tiled=True),
        lax.all_gather(row_delta, "blk", axis=0, tiled=True),
    )

    def add_queries(totals, pieces, first_row):
        query_piece, grad_piece = pieces
        piece_rows = query_piece.shape[0]
        for offset_rows in range(0, piece_rows, 512):
            span_rows = min(512, piece_rows - offset_rows)
            start_row = first_row + offset_rows
            span_block = lax.dynamic_slice_in_dim(row_block, start_row, span_rows)
            span_copy = lax.dynamic_slice_in_dim(row_copy, start_row, span_rows)
            reaches = (own_block < span_block) | (own_block == span_block) & (span_copy == 1)
            allowed = jnp.broadcast_to(reaches[:, None], (span_rows, half_rows))
            compute = partial(
                tile_grads,
                query_piece[offset_rows : offset_rows + span_rows],
                grad_piece[offset_rows : offset_rows + span_rows],
                lax.dynamic_slice_in_dim(every_lse, start_row, span_rows),
                lax.dynamic_slice_in_dim(every_delta, start_row, span_rows),
                clean_keys,
                clean_values,
                allowed,
                False,
                True,
            )
            results = compute()
            totals = (totals[0] + results[0], totals[1] + results[1])
        return totals

    clean_dkey, clean_dvalue = add_queries(
        (jnp.zeros(clean_shape, jnp.float32), jnp.zeros(clean_shape, jnp.float32)),
        (
            lax.all_gather(queries, "blk", axis=0, tiled=True),
            lax.all_gather(grad_rows, "blk", axis=0, tiled=True),
        ),
        jnp.int32(0),
    )
    noisy_query = queries[noisy_rows]
    noisy_grad = grad_rows[noisy_rows]
    noisy_lse = saved_lse[noisy_rows]
    noisy_delta = row_delta[noisy_rows]
    noisy_keys = key_rows[noisy_rows]
    noisy_values = value_rows[noisy_rows]
    reach = BLOCK // half_rows
    noisy_dquery = jnp.zeros(clean_shape, jnp.float32)
    noisy_dkey = jnp.zeros(clean_shape, jnp.float32)
    noisy_dvalue = jnp.zeros(clean_shape, jnp.float32)
    offsets = [0] + list(range(1, reach)) + [-distance for distance in range(1, reach)]
    for offset in offsets:
        if offset == 0:
            peer_keys, peer_values = (noisy_keys, noisy_values)
            active = jnp.array(True)
        else:
            peer_keys, peer_values = shifted((noisy_keys, noisy_values), "blk", offset)
            source = my_index - offset
            inside = (source >= 0) & (source < cycle_size)
            active = inside & (shard_block[jnp.clip(source, 0, cycle_size - 1)] == own_block)
        allowed = jnp.broadcast_to(active, (half_rows, half_rows))
        compute = partial(
            tile_grads,
            noisy_query,
            noisy_grad,
            noisy_lse,
            noisy_delta,
            peer_keys,
            peer_values,
            allowed,
            True,
            True,
        )
        results = compute()
        noisy_dquery = noisy_dquery + results[0]
        if offset == 0:
            noisy_dkey = results[1]
            noisy_dvalue = results[2]
        else:
            returned_dkey, returned_dvalue = (
                shifted(results[1].astype(jnp.bfloat16), "blk", -offset).astype(jnp.float32),
                shifted(results[2].astype(jnp.bfloat16), "blk", -offset).astype(jnp.float32),
            )
            noisy_dkey = noisy_dkey + returned_dkey
            noisy_dvalue = noisy_dvalue + returned_dvalue
    grad_query = grad_query.at[noisy_rows].add(noisy_dquery)
    grad_keys = (
        jnp.zeros(head_shape, jnp.float32)
        .at[clean_rows]
        .set(clean_dkey)
        .at[noisy_rows]
        .set(noisy_dkey)
    )
    grad_values = (
        jnp.zeros(head_shape, jnp.float32)
        .at[clean_rows]
        .set(clean_dvalue)
        .at[noisy_rows]
        .set(noisy_dvalue)
    )

    def to_rows(tensor):
        return tensor.astype(jnp.bfloat16).reshape(shard_rows, local_heads * HD)

    return (
        lax.all_to_all(to_rows(grad_query), "head", split_axis=0, concat_axis=1, tiled=True),
        lax.all_to_all(to_rows(grad_keys), "head", split_axis=0, concat_axis=1, tiled=True),
        lax.all_to_all(to_rows(grad_values), "head", split_axis=0, concat_axis=1, tiled=True),
    )


def solution(mesh):
    in_specs = (
        P(("blk", "head"), None),
        P(("blk", "head"), None),
        P(("blk", "head"), None),
        P(("blk", "head"), None),
        P(("blk", "head"), None),
        P("blk", "head"),
        P(),
        P(),
    )
    out_specs = (P(("blk", "head"), None), P(("blk", "head"), None), P(("blk", "head"), None))
    return jax.shard_map(
        per_device, mesh=mesh, in_specs=in_specs, out_specs=out_specs, check_vma=False
    )
```

profile of v0, /device:TPU:10, one launch (start us, length us, event | category | flops | bytes accessed | tf_op | source)
XLA Modules:
  0.0 702.5 jit_solution(10161836055062059991)
XLA Ops:
  8.7 5.9 all-to-all-start
  15.4 2.5 sort.17
  23.0 8.6 %all_to_all.134 = bf16[32,4,512]{2,0,1:T(8,128)(2,1)S(1)} all-to-all(bf16[32,4,512]{2,0,1:T(8,128)(2,1)S(1)} %bitcast.380), channel_id=1, replica_groups=mesh['blk'=64,'head'=4] {'head'}, dimensions={1} | all-to-all | bytes 262144 | tf_op jit(solution)/shard_map/all_to_all | solution.py:57
  33.9 8.4 %all_to_all.135 = bf16[32,4,512]{2,0,1:T(8,128)(2,1)S(1)} all-to-all(bf16[32,4,512]{2,0,1:T(8,128)(2,1)S(1)} %bitcast.381), channel_id=1, replica_groups=mesh['blk'=64,'head'=4] {'head'}, dimensions={1} | all-to-all | bytes 262144 | tf_op jit(solution)/shard_map/all_to_all | solution.py:55
  44.7 3.3 all-to-all-start.3
  50.5 4.4 compare_select_fusion.1
  56.5 5.1 all-to-all-start.4
  62.3 102.0 %all_gather.21 = f32[8192,4]{0,1:T(4,128)S(1)} all-gather(f32[128,4]{0,1:T(4,128)} %param.15), channel_id=1, replica_groups=mesh['blk'=64,'head'=4] {'blk'}, dimensions={0}, use_global_device_ids=true | all-gather | bytes 133120 | tf_op jit(solution)/shard_map/all_gather | solution.py:112
  179.1 2.9 compare_reduce_fusion.56
  182.1 37.2 %select_select_fusion = s32[4096]{0:T(1024)S(1)} fusion(pred[4096]{0:T(1024)(128)(4,1)S(1)} %get-tuple-element.73, pred[4096]{0:T(1024)(128)(4,1)S(1)} %get-tuple-element.72, pred[4096]{0:T(1024)(128)(4,1)S(1)} %get-tuple-element.71, pred[4096]{0:T(1024)(128)(4,1)S(1)} %get-tuple-element.70, pred[4096]{0:T(1024)(128)(4,1)S(1)} %get-tuple-element.69, ...), kind=kLoop, calls=%fused_computation.588 | loop fusion | flops 270336 | bytes 282980 | tf_op jit(solution)/shard_map/jit(_take)/select_n | solution.py:79
  238.9 3.3 collective-permute-start.4
  243.2 149.6 %all_gather.23 = f32[8192,4]{1,0:T(8,128)S(1)} all-gather(f32[128,4]{1,0:T(8,128)S(1)} %multiply_reduce_fusion), channel_id=1, replica_groups=mesh['blk'=64,'head'=4] {'blk'}, dimensions={0}, use_global_device_ids=true | all-gather | bytes 133120 | tf_op jit(solution)/shard_map/all_gather | solution.py:113
  416.9 4.0 collective-permute-start.7
  422.1 9.9 %collective-permute-start.8 = (bf16[64,4,128]{2,0,1:T(8,128)(2,1)}, bf16[64,4,128]{2,0,1:T(8,128)(2,1)S(1)}, u32[]{:S(2)}, u32[]{:S(2)}) collective-permute-start(bf16[64,4,128]{2,0,1:T(8,128)(2,1)} %copy.241), channel_id=1, source_target_pairs={{8,0},{12,4},{16,8},{20,12},{24,16},{28,20},{32,24},{36,28},{40,32... | collective-permute-start | bytes 196616 | tf_op jit(solution)/shard_map/ppermute | solution.py:15
  436.5 8.9 %collective-permute-start.10 = (bf16[64,4,128]{2,0,1:T(8,128)(2,1)}, bf16[64,4,128]{2,0,1:T(8,128)(2,1)S(1)}, u32[]{:S(2)}, u32[]{:S(2)}) collective-permute-start(bf16[64,4,128]{2,0,1:T(8,128)(2,1)} %copy.241), channel_id=1, source_target_pairs={{12,0},{16,4},{20,8},{24,12},{28,16},{32,20},{36,24},{40,28},{44,3... | collective-permute-start | bytes 196616 | tf_op jit(solution)/shard_map/ppermute | solution.py:15
  449.1 2.8 collective-permute-start.12
  453.1 9.1 %collective-permute-start.13 = (bf16[64,4,128]{2,0,1:T(8,128)(2,1)S(1)}, bf16[64,4,128]{2,0,1:T(8,128)(2,1)S(1)}, u32[]{:S(2)}, u32[]{:S(2)}) collective-permute-start(bf16[64,4,128]{2,0,1:T(8,128)(2,1)S(1)} %fusion.244), channel_id=1, source_target_pairs={{8,0},{12,4},{16,8},{20,12},{24,16},{28,20},{32,24},{36,28},{40,32... | collective-permute-start | bytes 196616 | tf_op jit(solution)/shard_map/ppermute | solution.py:15
  463.4 3.5 collective-permute-start.14
  469.6 2.6 collective-permute-start.16
  474.7 3.7 collective-permute-start.17
  480.7 10.2 %collective-permute-start.19 = (bf16[64,4,128]{2,0,1:T(8,128)(2,1)S(1)}, bf16[64,4,128]{2,0,1:T(8,128)(2,1)S(1)}, u32[]{:S(2)}, u32[]{:S(2)}) collective-permute-start(bf16[64,4,128]{2,0,1:T(8,128)(2,1)S(1)} %fusion.235), channel_id=1, source_target_pairs={{8,0},{12,4},{16,8},{20,12},{24,16},{28,20},{32,24},{36,28},{40,32... | collective-permute-start | bytes 196616 | tf_op jit(solution)/shard_map/ppermute | solution.py:15
  493.1 2.5 collective-permute-start.21
  495.6 3.2 collective-permute-start.22
  498.9 2.6 collective-permute-start.23
  502.6 10.9 %collective-permute-done.23 = bf16[64,4,128]{2,0,1:T(8,128)(2,1)S(1)} collective-permute-done((bf16[64,4,128]{2,0,1:T(8,128)(2,1)S(1)}, bf16[64,4,128]{2,0,1:T(8,128)(2,1)S(1)}, u32[]{:S(2)}, u32[]{:S(2)}) %collective-permute-start.23) | collective-permute-done | bytes 65568 | tf_op jit(solution)/shard_map/ppermute | solution.py:15
  514.4 3.1 fusion.545
  533.0 4.1 fusion.544
  537.1 2.8 fusion.60
  539.9 2.6 fusion.61
  542.5 2.7 fusion.62
  545.2 2.7 fusion.59
  555.9 2.7 scatter_fusion
  559.4 14.7 %all-to-all-start.5 = ((bf16[4,32,512]{2,1,0:T(8,128)(2,1)}), bf16[4,32,512]{2,1,0:T(8,128)(2,1)}, u32[]{:S(2)}, u32[]{:S(2)}) async-start(bf16[4,32,512]{2,1,0:T(8,128)(2,1)} %all_to_all.114), calls=%async_computation.5 | async-start | bytes 262144 | tf_op jit(solution)/shard_map/all_to_all | solution.py:215
  593.5 2.5 fusion.151
  602.7 2.4 fusion.153
  611.1 2.4 fusion.145
  615.7 2.4 fusion.154
  620.3 2.5 fusion.155
  624.9 2.5 fusion.156
  629.5 2.5 fusion.157
  634.1 2.4 fusion.158
  638.8 3.0 fusion.220
  643.4 4.7 scatter_fusion.1
  648.1 2.6 scatter_fusion.2
  671.9 5.1 all-to-all-start.6
  678.4 2.4 scatter_fusion.3
  684.1 5.1 all-to-all-start.7
  691.4 3.7 all-to-all-done.7
  (335 shorter events, 191.3 us)
Async XLA Ops:
  8.7 12.0 %all-to-all-start = ((bf16[32,4,512]{2,0,1:T(8,128)(2,1)}), bf16[32,4,512]{2,0,1:T(8,128)(2,1)S(1)}, u32[]{:S(2)}, u32[]{:S(2)}) async-start(bf16[32,4,512]{2,0,1:T(8,128)(2,1)} %bitcast.371), calls=%async_computation | async-start | bytes 262144 | tf_op jit(solution)/shard_map/all_to_all | solution.py:56
  14.6 499.8 %all-gather.11.cloned.1.call-start = ((), (), s32[]{:S(2)}) async-start(), calls=%async_computation.10 | async-start | bytes 4259840 | tf_op jit(solution)/shard_map/all_gather | solution.py:83
  18.0 38.5 %copy-start.35 = (s32[64]{0:T(128)}, s32[64]{0:T(128)S(1)}, u32[]{:S(2)}) copy-start(s32[64]{0:T(128)S(1)} %get-tuple-element.231) | copy-start | bytes 772
  22.0 511.0 %all-gather.13.cloned.1.call-start = ((), (), s32[]{:S(2)}) async-start(), calls=%async_computation.11 | async-start | bytes 4259840 | tf_op jit(solution)/shard_map/all_gather | solution.py:84
  33.0 541.1 %all-gather.7.cloned.1.call-start = ((), (), s32[]{:S(2)}) async-start(), calls=%async_computation.8 | async-start | bytes 8519680 | tf_op jit(solution)/shard_map/all_gather | solution.py:145
  42.4 199.8 %copy-start.11 = (bf16[128,4,128]{2,1,0:T(4,128)(2,1)}, bf16[128,4,128]{2,1,0:T(4,128)(2,1)S(1)}, u32[]{:S(2)}) copy-start(bf16[128,4,128]{2,1,0:T(4,128)(2,1)S(1)} %reshape.538) | copy-start | bytes 393220
  44.7 11.8 %all-to-all-start.3 = ((bf16[32,4,512]{2,0,1:T(8,128)(2,1)}), bf16[32,4,512]{2,0,1:T(8,128)(2,1)S(1)}, u32[]{:S(2)}, u32[]{:S(2)}) async-start(bf16[32,4,512]{2,0,1:T(8,128)(2,1)} %bitcast.368), calls=%async_computation.3 | async-start | bytes 262144 | tf_op jit(solution)/shard_map/all_to_all | solution.py:59
  56.5 185.7 %all-to-all-start.4 = ((bf16[32,4,512]{2,0,1:T(8,128)(2,1)}), bf16[32,4,512]{2,0,1:T(8,128)(2,1)S(1)}, u32[]{:S(2)}, u32[]{:S(2)}) async-start(bf16[32,4,512]{2,0,1:T(8,128)(2,1)} %bitcast.367), calls=%async_computation.4 | async-start | bytes 262144 | tf_op jit(solution)/shard_map/all_to_all | solution.py:58
  61.5 515.4 %all-gather.9.cloned.1.call-start = ((), (), s32[]{:S(2)}) async-start(), calls=%async_computation.9 | async-start | bytes 8519680 | tf_op jit(solution)/shard_map/all_gather | solution.py:146
  165.7 227.3 %copy-start.49 = (f32[4,64]{1,0:T(4,128)}, f32[4,64]{1,0:T(4,128)S(1)}, u32[]{:S(2)}) copy-start(f32[4,64]{1,0:T(4,128)S(1)} %copy.237) | copy-start | bytes 3076
  228.3 164.8 %copy-start.13 = (bf16[64,4,128]{2,1,0:T(4,128)(2,1)}, bf16[64,4,128]{2,1,0:T(4,128)(2,1)S(1)}, u32[]{:S(2)}) copy-start(bf16[64,4,128]{2,1,0:T(4,128)(2,1)S(1)} %gather_fusion.2) | copy-start | bytes 196612
  230.2 180.3 %collective-permute-start = (bf16[64,4,128]{2,0,1:T(8,128)(2,1)}, bf16[64,4,128]{2,0,1:T(8,128)(2,1)}, u32[]{:S(2)}, u32[]{:S(2)}) collective-permute-start(bf16[64,4,128]{2,0,1:T(8,128)(2,1)} %copy.241), channel_id=1, source_target_pairs={{0,4},{4,8},{8,12},{12,16},{16,20},{20,24},{24,28},{28,32},{32,36}... | collective-permute-start | bytes 196616 | tf_op jit(solution)/shard_map/ppermute | solution.py:15
  232.5 181.2 %collective-permute-start.2 = (bf16[64,4,128]{2,0,1:T(8,128)(2,1)}, bf16[64,4,128]{2,0,1:T(8,128)(2,1)}, u32[]{:S(2)}, u32[]{:S(2)}) collective-permute-start(bf16[64,4,128]{2,0,1:T(8,128)(2,1)} %copy.241), channel_id=1, source_target_pairs={{0,8},{4,12},{8,16},{12,20},{16,24},{20,28},{24,32},{28,36},{32,40... | collective-permute-start | bytes 196616 | tf_op jit(solution)/shard_map/ppermute | solution.py:15
  235.0 210.9 %collective-permute-start.1 = (bf16[64,4,128]{2,0,1:T(8,128)(2,1)}, bf16[64,4,128]{2,0,1:T(8,128)(2,1)}, u32[]{:S(2)}, u32[]{:S(2)}) collective-permute-start(bf16[64,4,128]{2,0,1:T(8,128)(2,1)} %copy.239), channel_id=1, source_target_pairs={{0,4},{4,8},{8,12},{12,16},{16,20},{20,24},{24,28},{28,32},{32,36}... | collective-permute-start | bytes 196616 | tf_op jit(solution)/shard_map/ppermute | solution.py:15
  236.9 212.1 %collective-permute-start.3 = (bf16[64,4,128]{2,0,1:T(8,128)(2,1)}, bf16[64,4,128]{2,0,1:T(8,128)(2,1)}, u32[]{:S(2)}, u32[]{:S(2)}) collective-permute-start(bf16[64,4,128]{2,0,1:T(8,128)(2,1)} %copy.239), channel_id=1, source_target_pairs={{0,8},{4,12},{8,16},{12,20},{16,24},{20,28},{24,32},{28,36},{32,40... | collective-permute-start | bytes 196616 | tf_op jit(solution)/shard_map/ppermute | solution.py:15
  238.9 178.0 %collective-permute-start.4 = (bf16[64,4,128]{2,0,1:T(8,128)(2,1)}, bf16[64,4,128]{2,0,1:T(8,128)(2,1)}, u32[]{:S(2)}, u32[]{:S(2)}) collective-permute-start(bf16[64,4,128]{2,0,1:T(8,128)(2,1)} %copy.241), channel_id=1, source_target_pairs={{0,12},{4,16},{8,20},{12,24},{16,28},{20,32},{24,36},{28,40},{32,4... | collective-permute-start | bytes 196616 | tf_op jit(solution)/shard_map/ppermute | solution.py:15
  403.3 69.2 %copy-start.15 = (f32[4,128,64]{1,2,0:T(8,128)S(1)}, f32[4,128,64]{1,2,0:T(8,128)}, u32[]{:S(2)}) copy-start(f32[4,128,64]{1,2,0:T(8,128)} %fusion.442) | copy-start | bytes 393220
  404.0 109.5 %copy-start.17 = (f32[4,64,64]{2,1,0:T(8,128)S(1)}, f32[4,64,64]{2,1,0:T(8,128)}, u32[]{:S(2)}) copy-start(f32[4,64,64]{2,1,0:T(8,128)} %copy-done.16) | copy-start | bytes 196612
  404.7 64.5 %copy-start.50 = (f32[4,64]{1,0:T(4,128)S(1)}, f32[4,64]{1,0:T(4,128)}, u32[]{:S(2)}) copy-start(f32[4,64]{1,0:T(4,128)} %copy-done.49) | copy-start | bytes 3076
  410.5 22.6 %collective-permute-start.5 = (bf16[64,4,128]{2,0,1:T(8,128)(2,1)}, bf16[64,4,128]{2,0,1:T(8,128)(2,1)S(1)}, u32[]{:S(2)}, u32[]{:S(2)}) collective-permute-start(bf16[64,4,128]{2,0,1:T(8,128)(2,1)} %copy.239), channel_id=1, source_target_pairs={{0,12},{4,16},{8,20},{12,24},{16,28},{20,32},{24,36},{28,40},{32,4... | collective-permute-start | bytes 196616 | tf_op jit(solution)/shard_map/ppermute | solution.py:15
  413.7 8.4 %collective-permute-start.6 = (bf16[64,4,128]{2,0,1:T(8,128)(2,1)}, bf16[64,4,128]{2,0,1:T(8,128)(2,1)S(1)}, u32[]{:S(2)}, u32[]{:S(2)}) collective-permute-start(bf16[64,4,128]{2,0,1:T(8,128)(2,1)} %copy.241), channel_id=1, source_target_pairs={{4,0},{8,4},{12,8},{16,12},{20,16},{24,20},{28,24},{32,28},{36,32}... | collective-permute-start | bytes 196616 | tf_op jit(solution)/shard_map/ppermute | solution.py:15
  416.9 19.6 %collective-permute-start.7 = (bf16[64,4,128]{2,0,1:T(8,128)(2,1)}, bf16[64,4,128]{2,0,1:T(8,128)(2,1)S(1)}, u32[]{:S(2)}, u32[]{:S(2)}) collective-permute-start(bf16[64,4,128]{2,0,1:T(8,128)(2,1)} %copy.239), channel_id=1, source_target_pairs={{4,0},{8,4},{12,8},{16,12},{20,16},{24,20},{28,24},{32,28},{36,32}... | collective-permute-start | bytes 196616 | tf_op jit(solution)/shard_map/ppermute | solution.py:15
  422.1 31.0 %collective-permute-start.8 = (bf16[64,4,128]{2,0,1:T(8,128)(2,1)}, bf16[64,4,128]{2,0,1:T(8,128)(2,1)S(1)}, u32[]{:S(2)}, u32[]{:S(2)}) collective-permute-start(bf16[64,4,128]{2,0,1:T(8,128)(2,1)} %copy.241), channel_id=1, source_target_pairs={{8,0},{12,4},{16,8},{20,12},{24,16},{28,20},{32,24},{36,28},{40,32... | collective-permute-start | bytes 196616 | tf_op jit(solution)/shard_map/ppermute | solution.py:15
  433.2 30.2 %collective-permute-start.9 = (bf16[64,4,128]{2,0,1:T(8,128)(2,1)}, bf16[64,4,128]{2,0,1:T(8,128)(2,1)S(1)}, u32[]{:S(2)}, u32[]{:S(2)}) collective-permute-start(bf16[64,4,128]{2,0,1:T(8,128)(2,1)} %copy.239), channel_id=1, source_target_pairs={{8,0},{12,4},{16,8},{20,12},{24,16},{28,20},{32,24},{36,28},{40,32... | collective-permute-start | bytes 196616 | tf_op jit(solution)/shard_map/ppermute | solution.py:15
  436.5 30.8 %collective-permute-start.10 = (bf16[64,4,128]{2,0,1:T(8,128)(2,1)}, bf16[64,4,128]{2,0,1:T(8,128)(2,1)S(1)}, u32[]{:S(2)}, u32[]{:S(2)}) collective-permute-start(bf16[64,4,128]{2,0,1:T(8,128)(2,1)} %copy.241), channel_id=1, source_target_pairs={{12,0},{16,4},{20,8},{24,12},{28,16},{32,20},{36,24},{40,28},{44,3... | collective-permute-start | bytes 196616 | tf_op jit(solution)/shard_map/ppermute | solution.py:15
  445.9 23.6 %collective-permute-start.11 = (bf16[64,4,128]{2,0,1:T(8,128)(2,1)}, bf16[64,4,128]{2,0,1:T(8,128)(2,1)S(1)}, u32[]{:S(2)}, u32[]{:S(2)}) collective-permute-start(bf16[64,4,128]{2,0,1:T(8,128)(2,1)} %copy.239), channel_id=1, source_target_pairs={{12,0},{16,4},{20,8},{24,12},{28,16},{32,20},{36,24},{40,28},{44,3... | collective-permute-start | bytes 196616 | tf_op jit(solution)/shard_map/ppermute | solution.py:15
  449.1 25.7 %collective-permute-start.12 = (bf16[64,4,128]{2,0,1:T(8,128)(2,1)S(1)}, bf16[64,4,128]{2,0,1:T(8,128)(2,1)S(1)}, u32[]{:S(2)}, u32[]{:S(2)}) collective-permute-start(bf16[64,4,128]{2,0,1:T(8,128)(2,1)S(1)} %fusion.245), channel_id=1, source_target_pairs={{4,0},{8,4},{12,8},{16,12},{20,16},{24,20},{28,24},{32,28},{36,32}... | collective-permute-start | bytes 196616 | tf_op jit(solution)/shard_map/ppermute | solution.py:15
  453.1 25.3 %collective-permute-start.13 = (bf16[64,4,128]{2,0,1:T(8,128)(2,1)S(1)}, bf16[64,4,128]{2,0,1:T(8,128)(2,1)S(1)}, u32[]{:S(2)}, u32[]{:S(2)}) collective-permute-start(bf16[64,4,128]{2,0,1:T(8,128)(2,1)S(1)} %fusion.244), channel_id=1, source_target_pairs={{8,0},{12,4},{16,8},{20,12},{24,16},{28,20},{32,24},{36,28},{40,32... | collective-permute-start | bytes 196616 | tf_op jit(solution)/shard_map/ppermute | solution.py:15
  463.4 17.3 %collective-permute-start.14 = (bf16[64,4,128]{2,0,1:T(8,128)(2,1)S(1)}, bf16[64,4,128]{2,0,1:T(8,128)(2,1)S(1)}, u32[]{:S(2)}, u32[]{:S(2)}) collective-permute-start(bf16[64,4,128]{2,0,1:T(8,128)(2,1)S(1)} %fusion.243), channel_id=1, source_target_pairs={{12,0},{16,4},{20,8},{24,12},{28,16},{32,20},{36,24},{40,28},{44,3... | collective-permute-start | bytes 196616 | tf_op jit(solution)/shard_map/ppermute | solution.py:15
  467.3 23.7 %collective-permute-start.15 = (bf16[64,4,128]{2,0,1:T(8,128)(2,1)S(1)}, bf16[64,4,128]{2,0,1:T(8,128)(2,1)S(1)}, u32[]{:S(2)}, u32[]{:S(2)}) collective-permute-start(bf16[64,4,128]{2,0,1:T(8,128)(2,1)S(1)} %fusion.242), channel_id=1, source_target_pairs={{0,4},{4,8},{8,12},{12,16},{16,20},{20,24},{24,28},{28,32},{32,36}... | collective-permute-start | bytes 196616 | tf_op jit(solution)/shard_map/ppermute | solution.py:15
  469.6 23.6 %collective-permute-start.16 = (bf16[64,4,128]{2,0,1:T(8,128)(2,1)S(1)}, bf16[64,4,128]{2,0,1:T(8,128)(2,1)S(1)}, u32[]{:S(2)}, u32[]{:S(2)}) collective-permute-start(bf16[64,4,128]{2,0,1:T(8,128)(2,1)S(1)} %fusion.241), channel_id=1, source_target_pairs={{0,8},{4,12},{8,16},{12,20},{16,24},{20,28},{24,32},{28,36},{32,40... | collective-permute-start | bytes 196616 | tf_op jit(solution)/shard_map/ppermute | solution.py:15
  472.5 50.4 %copy-start.38 = (f32[128,4]{0,1:T(4,128)S(1)}, f32[128,4]{0,1:T(4,128)}, u32[]{:S(2)}) copy-start(f32[128,4]{0,1:T(4,128)} %param.15) | copy-start | bytes 6148
  474.7 20.9 %collective-permute-start.17 = (bf16[64,4,128]{2,0,1:T(8,128)(2,1)S(1)}, bf16[64,4,128]{2,0,1:T(8,128)(2,1)S(1)}, u32[]{:S(2)}, u32[]{:S(2)}) collective-permute-start(bf16[64,4,128]{2,0,1:T(8,128)(2,1)S(1)} %fusion.240), channel_id=1, source_target_pairs={{0,12},{4,16},{8,20},{12,24},{16,28},{20,32},{24,36},{28,40},{32,4... | collective-permute-start | bytes 196616 | tf_op jit(solution)/shard_map/ppermute | solution.py:15
  478.4 20.4 %collective-permute-start.18 = (bf16[64,4,128]{2,0,1:T(8,128)(2,1)S(1)}, bf16[64,4,128]{2,0,1:T(8,128)(2,1)S(1)}, u32[]{:S(2)}, u32[]{:S(2)}) collective-permute-start(bf16[64,4,128]{2,0,1:T(8,128)(2,1)S(1)} %fusion.234), channel_id=1, source_target_pairs={{4,0},{8,4},{12,8},{16,12},{20,16},{24,20},{28,24},{32,28},{36,32}... | collective-permute-start | bytes 196616 | tf_op jit(solution)/shard_map/ppermute | solution.py:15
  480.7 21.8 %collective-permute-start.19 = (bf16[64,4,128]{2,0,1:T(8,128)(2,1)S(1)}, bf16[64,4,128]{2,0,1:T(8,128)(2,1)S(1)}, u32[]{:S(2)}, u32[]{:S(2)}) collective-permute-start(bf16[64,4,128]{2,0,1:T(8,128)(2,1)S(1)} %fusion.235), channel_id=1, source_target_pairs={{8,0},{12,4},{16,8},{20,12},{24,16},{28,20},{32,24},{36,28},{40,32... | collective-permute-start | bytes 196616 | tf_op jit(solution)/shard_map/ppermute | solution.py:15
  491.0 11.6 %collective-permute-start.20 = (bf16[64,4,128]{2,0,1:T(8,128)(2,1)S(1)}, bf16[64,4,128]{2,0,1:T(8,128)(2,1)S(1)}, u32[]{:S(2)}, u32[]{:S(2)}) collective-permute-start(bf16[64,4,128]{2,0,1:T(8,128)(2,1)S(1)} %fusion.236), channel_id=1, source_target_pairs={{12,0},{16,4},{20,8},{24,12},{28,16},{32,20},{36,24},{40,28},{44,3... | collective-permute-start | bytes 196616 | tf_op jit(solution)/shard_map/ppermute | solution.py:15
  493.1 9.4 %collective-permute-start.21 = (bf16[64,4,128]{2,0,1:T(8,128)(2,1)S(1)}, bf16[64,4,128]{2,0,1:T(8,128)(2,1)S(1)}, u32[]{:S(2)}, u32[]{:S(2)}) collective-permute-start(bf16[64,4,128]{2,0,1:T(8,128)(2,1)S(1)} %fusion.237), channel_id=1, source_target_pairs={{0,4},{4,8},{8,12},{12,16},{16,20},{20,24},{24,28},{28,32},{32,36}... | collective-permute-start | bytes 196616 | tf_op jit(solution)/shard_map/ppermute | solution.py:15
  495.6 6.9 collective-permute-start.22
  498.9 14.6 %collective-permute-start.23 = (bf16[64,4,128]{2,0,1:T(8,128)(2,1)S(1)}, bf16[64,4,128]{2,0,1:T(8,128)(2,1)S(1)}, u32[]{:S(2)}, u32[]{:S(2)}) collective-permute-start(bf16[64,4,128]{2,0,1:T(8,128)(2,1)S(1)} %fusion.239), channel_id=1, source_target_pairs={{0,12},{4,16},{8,20},{12,24},{16,28},{20,32},{24,36},{28,40},{32,4... | collective-permute-start | bytes 196616 | tf_op jit(solution)/shard_map/ppermute | solution.py:15
  553.5 32.5 %copy-start.33 = (f32[4,512]{1,0:T(4,128)S(1)}, f32[4,512]{1,0:T(4,128)}, u32[]{:S(2)}) copy-start(f32[4,512]{1,0:T(4,128)} %copy.303) | copy-start | bytes 24580
  555.7 32.6 %copy-start.19 = (bf16[64,4,128]{2,1,0:T(4,128)(2,1)S(1)}, bf16[64,4,128]{2,1,0:T(4,128)(2,1)}, u32[]{:S(2)}) copy-start(bf16[64,4,128]{2,1,0:T(4,128)(2,1)} %gather_fusion) | copy-start | bytes 196612
  555.7 32.6 %copy-start.47 = (f32[4,512]{1,0:T(4,128)S(1)}, f32[4,512]{1,0:T(4,128)}, u32[]{:S(2)}) copy-start(f32[4,512]{1,0:T(4,128)} %get-tuple-element.117) | copy-start | bytes 24580
  555.7 32.6 %copy-start.53 = (pred[512]{0:T(512)(128)(4,1)S(1)}, pred[512]{0:T(512)(128)(4,1)}, u32[]{:S(2)}) copy-start(pred[512]{0:T(512)(128)(4,1)} %get-tuple-element.131) | copy-start | bytes 1540
  555.7 34.0 %copy-start.32 = (f32[4,512]{1,0:T(4,128)S(1)}, f32[4,512]{1,0:T(4,128)}, u32[]{:S(2)}) copy-start(f32[4,512]{1,0:T(4,128)} %copy.300) | copy-start | bytes 24580
  559.4 34.0 %copy-start.31 = (f32[4,512]{1,0:T(4,128)S(1)}, f32[4,512]{1,0:T(4,128)}, u32[]{:S(2)}) copy-start(f32[4,512]{1,0:T(4,128)} %copy.297) | copy-start | bytes 24580
  559.4 112.5 %all-to-all-start.5 = ((bf16[4,32,512]{2,1,0:T(8,128)(2,1)}), bf16[4,32,512]{2,1,0:T(8,128)(2,1)}, u32[]{:S(2)}, u32[]{:S(2)}) async-start(bf16[4,32,512]{2,1,0:T(8,128)(2,1)} %all_to_all.114), calls=%async_computation.5 | async-start | bytes 262144 | tf_op jit(solution)/shard_map/all_to_all | solution.py:215
  671.9 12.2 %all-to-all-start.6 = ((bf16[4,32,512]{2,1,0:T(8,128)(2,1)}), bf16[4,32,512]{2,1,0:T(8,128)(2,1)S(1)}, u32[]{:S(2)}, u32[]{:S(2)}) async-start(bf16[4,32,512]{2,1,0:T(8,128)(2,1)} %all_to_all.118), calls=%async_computation.6 | async-start | bytes 262144 | tf_op jit(solution)/shard_map/all_to_all | solution.py:216
  684.1 11.0 %all-to-all-start.7 = ((bf16[4,32,512]{2,1,0:T(8,128)(2,1)}), bf16[4,32,512]{2,1,0:T(8,128)(2,1)S(1)}, u32[]{:S(2)}, u32[]{:S(2)}) async-start(bf16[4,32,512]{2,1,0:T(8,128)(2,1)} %all_to_all.122), calls=%async_computation.7 | async-start | bytes 262144 | tf_op jit(solution)/shard_map/all_to_all | solution.py:217
  (45 other events, 842.5 us)
Sparse Core Ops, SparseCore 0:
  22.1 91.9 all-gather.10
  117.7 86.8 all-gather.12
  208.3 130.2 all-gather.6
  342.8 121.6 all-gather.8
where the time goes:
time: 712 us; the launch traced here: 702 us
  blocking collectives  269 us (38%)
  matrix products  137 us (19%)
  starting transfers between devices  127 us (18%)
  local copies, waits for them, and re-layouts  71.2 us (10%)
  other arithmetic  58.8 us (8%)
  between operations  22.5 us (3%)
  waiting for transfers between devices  16.9 us (2%)
    all_gather x1, blocking collectives, per_device(): lax.all_gather(row_delta, 'blk', axis=0, tiled=True)  150 us
    all_gather x1, blocking collectives, per_device(): lax.all_gather(saved_lse, 'blk', axis=0, tiled=True)  102 us
    ppermute x24, starting transfers between devices, shifted(): return lax.ppermute(block, axis, route)  88.2 us
    dot_general x31, matrix products, tile_grads(): jnp.einsum('qhd,khd->hqk', queries, key_rows, preferred_element_type=jnp....  48.8 us
    dot_general x23, matrix products, tile_grads(): jnp.einsum('hqk,qhd->khd', dscores, queries, preferred_element_type=jnp.f...  39.7 us
    select_n x1, other arithmetic, per_device(): jnp.repeat(shard_block, half_rows, total_repeat_length=cycle_size * half_...  37.2 us
    dot_general x23, matrix products, tile_grads(): jnp.einsum('hqk,qhd->khd', weights.astype(jnp.bfloat16), grad_rows, prefe...  23 us
    dot_general x15, matrix products, tile_grads(): jnp.einsum('hqk,khd->qhd', dscores, key_rows, preferred_element_type=jnp....  22.7 us
  transfers between devices with their start and end apart: 34, of which 3 were waited for; matrix products, arithmetic and copies ran while one was open for 37% of the time, Pallas kernels for 0%

commit v1 on v0

v1 whole, which is shorter than its diff:
```python
import functools

import jax
import jax.numpy as jnp
from jax import lax
from jax.experimental import pallas as pl
from jax.experimental.pallas import tpu as pltpu
from jax.sharding import Mesh
from jax.sharding import PartitionSpec as P

HD = 128
RUN = 128
HALF = RUN // 2
AXES = ("y", "zh", "xh", "xl", "c", "zl")
SIZES = (4, 2, 2, 2, 2, 4)
HEAD_AXES = ("zh", "c", "zl")
QUERY_AXES = ("xh", "xl")
KEY_AXES = ("y",)
RUNS = 4
SCALE = HD**-0.5
LOG2E = 1.4426950408889634
F32 = jnp.float32
BF16 = jnp.bfloat16
VMEM = pl.BlockSpec(memory_space=pltpu.VMEM)
SMEM = pl.BlockSpec(memory_space=pltpu.SMEM)


def iota(shape, axis):
    return lax.broadcasted_iota(jnp.int32, shape, axis)


def split_two(x):
    high = x.astype(BF16).astype(F32)
    return high, x - high


def contract(a, b, dim_a, dim_b):
    return lax.dot_general(a, b, (((dim_a,), (dim_b,)), ((), ())), preferred_element_type=F32)


def call(body, out_shape, args, smem=(), scratch=(), limit=32 << 20, cost=None):
    return pl.pallas_call(
        body,
        out_shape=out_shape,
        in_specs=[SMEM if i in smem else VMEM for i in range(len(args))],
        out_specs=jax.tree.map(lambda _: VMEM, out_shape),
        scratch_shapes=list(scratch),
        compiler_params=pltpu.CompilerParams(vmem_limit_bytes=limit),
        cost_estimate=cost,
    )(*args)


def pack_kernel(q_ref, k_ref, v_ref, o_ref, g_ref, lse_ref, out_ref):
    rows = q_ref.shape[0]
    lane = iota((rows, 128), 1)
    delta = jnp.zeros((rows, 128), F32)
    for h in range(16):
        cols = slice(h * HD, (h + 1) * HD)
        term = g_ref[:, cols].astype(F32) * o_ref[:, cols].astype(F32)
        delta = jnp.where(lane == h, jnp.sum(term, axis=1, keepdims=True), delta)
    delta = jnp.concatenate([delta, jnp.zeros((128 - rows, 128), F32)], axis=0).T
    delta_high, delta_low = split_two(delta)
    lse_high, lse_low = split_two(lse_ref[...])
    row = iota((16, 128), 0)
    for slot in range(16):
        j, z = divmod(slot, 4)
        h = 4 * z + j
        cols = slice(h * HD, (h + 1) * HD)
        for i, ref in enumerate((q_ref, g_ref, k_ref, v_ref)):
            out_ref[slot, i * rows : (i + 1) * rows, :] = ref[:, cols]
        stats = jnp.where(row == 0, lse_high[j : j + 1], 0.0)
        stats = jnp.where(row == 1, lse_low[j : j + 1], stats)
        stats = jnp.where(row == 2, delta_high[h : h + 1], stats)
        stats = jnp.where(row == 3, delta_low[h : h + 1], stats)
        out_ref[slot, 4 * rows : 4 * rows + 16, :] = stats.astype(BF16)


def placing(copy_ref, j):
    zh, c = divmod(j, 2)
    shard = ((lax.axis_index("y") * 2 + zh) * 4 + lax.axis_index("xh") * 2 + lax.axis_index("xl")) * 2 + c
    copy = jnp.broadcast_to(copy_ref[pl.ds(shard, 1), :], (8, RUN)).astype(F32)
    upto = (iota((RUN, RUN), 0) <= iota((RUN, RUN), 1)).astype(BF16)
    count = contract(copy.astype(BF16), upto, 1, 0)
    index = iota((8, RUN), 1).astype(F32)
    place = jnp.where(copy > 0.5, HALF - 1.0 + count, index - count)
    place = jnp.broadcast_to(place[0:1], (RUN, RUN)).astype(jnp.int32)
    return (iota((RUN, RUN), 0) == place).astype(F32)


def sort_kernel(got_ref, copy_ref, qd_ref, kv_ref, kvn_ref):
    zl = lax.axis_index("zl")
    row = iota((16, RUN), 0)
    stats = []
    for j in range(RUNS):
        zh, c = divmod(j, 2)
        one_hot = placing(copy_ref, j).astype(BF16)
        parts = [
            jnp.concatenate([got_ref[4 * j + z, 32 * i : 32 * i + 32, :] for z in range(4)], axis=0)
            for i in range(4)
        ]
        moved = contract(one_hot, jnp.concatenate(parts, axis=1), 1, 0).astype(BF16)
        qd_ref[256 * zh + 64 * c : 256 * zh + 64 * c + 64, :] = moved[:HALF, :256]
        qd_ref[256 * zh + 128 + 64 * c : 256 * zh + 192 + 64 * c, :] = moved[HALF:, :256]
        kvn_ref[128 * zh + 64 * c : 128 * zh + 64 * c + 64, :] = moved[:HALF, 256:]
        kv_ref[128 * zh + 64 * c : 128 * zh + 64 * c + 64, :] = moved[HALF:, 256:]
        lse = got_ref[4 * j + zl, 128:144, :].astype(F32)
        delta = jnp.concatenate(
            [got_ref[4 * j + z, 128:144, :].astype(F32)[:, :32] for z in range(4)], axis=1
        )
        both = jnp.where(row < 2, lse, delta).astype(BF16)
        stats.append(contract(both, one_hot, 1, 1))
    halves = []
    for zh in range(2):
        a, b = stats[2 * zh], stats[2 * zh + 1]
        halves.append(
            jnp.concatenate([a[:8, :HALF], b[:8, :HALF], a[:8, HALF:], b[:8, HALF:]], axis=1)
        )
    qd_ref[512:528, :] = jnp.concatenate(halves, axis=0).astype(BF16)


def tile(k, kt, v, q, g, lse, delta):
    scores = contract(k, q, 1, 1)
    weights = jnp.exp2(scores * (SCALE * LOG2E) - lse)
    dweights = contract(v, g, 1, 1)
    dscores = (weights * (dweights - delta)).astype(BF16)
    dv = contract(weights.astype(BF16), g, 1, 0)
    dk = contract(dscores, q, 1, 0)
    dq = contract(kt, dscores, 1, 0)
    return dv, dk, dq


def attend_kernel(
    ids_ref, qd0, qd1, qd2, qd3, kv0, kv1, kv2, kv3, kvn_ref,
    dq0, dq1, dq2, dq3, dkv0, dkv1, dkv2, dkv3, dkvn_ref,
    q_all, g_all, lse_all, delta_all, k_all, kt_all, v_all, dqt, dk_all, dv_all,
):
    y, xh = lax.axis_index("y"), lax.axis_index("xh")
    for m, ref in enumerate((qd0, qd1, qd2, qd3)):
        stats = ref[512:528, :].astype(F32)
        for zh in range(2):
            block, at = zh * 2 + m // 2, 256 * (m % 2)
            q_all[block, at : at + 256, :] = ref[256 * zh : 256 * zh + 256, :HD]
            g_all[block, at : at + 256, :] = ref[256 * zh : 256 * zh + 256, HD:]
            s = 8 * zh
            lse_all[block, :, at : at + 256] = (stats[s : s + 1] + stats[s + 1 : s + 2]) * LOG2E
            delta_all[block, :, at : at + 256] = stats[s + 2 : s + 3] + stats[s + 3 : s + 4]
    for d, ref in enumerate((kv0, kv1, kv2, kv3)):
        for zh in range(2):
            n = 2 * d + zh
            k = ref[128 * zh : 128 * zh + 128, :HD]
            k_all[n] = k
            kt_all[n] = k.astype(F32).T.astype(BF16)
            v_all[n] = ref[128 * zh : 128 * zh + 128, HD:]
    dk_all[...] = jnp.zeros_like(dk_all)
    dv_all[...] = jnp.zeros_like(dv_all)

    for zh in range(2):
        block, n = zh * 2, zh
        kn = kvn_ref[128 * zh : 128 * zh + 128, :HD]
        vn = kvn_ref[128 * zh : 128 * zh + 128, HD:]
        knt = kn.astype(F32).T.astype(BF16)
        for copy in range(2):
            first, second = 128 * copy, 256 + 128 * copy

            def rows(ref):
                return jnp.concatenate([ref[block, first : first + 128, :], ref[block, second : second + 128, :]], axis=0)

            def lanes(ref):
                return jnp.concatenate([ref[block, :, first : first + 128], ref[block, :, second : second + 128]], axis=1)

            q, g, lse, delta = rows(q_all), rows(g_all), lanes(lse_all), lanes(delta_all)
            if copy == 0:
                dv, dk, dq = tile(kn, knt, vn, q, g, lse, delta)
                dkvn_ref[128 * zh : 128 * zh + 128, :] = jnp.concatenate([dk * SCALE, dv], axis=1).astype(BF16)
            else:
                dv, dk, dq = tile(k_all[n], kt_all[n], v_all[n], q, g, lse, delta)
                dk_all[n] = dk
                dv_all[n] = dv
            dqt[block, :, first : first + 128] = dq[:, :128]
            dqt[block, :, second : second + 128] = dq[:, 128:]
    for zh in range(2):
        dqt[zh * 2 + 1] = jnp.zeros((HD, 512), F32)

    for block in range(4):
        zq, other = divmod(block, 2)
        own_id = ids_ref[(y * 2 + zq) * 2 + (xh ^ other)]

        def step(n, carry, block=block, own_id=own_id):
            key_id = ids_ref[((y ^ (n // 2)) * 2 + n % 2) * 2 + xh]

            @pl.when(key_id < own_id)
            def _():
                dv, dk, dq = tile(
                    k_all[n], kt_all[n], v_all[n], q_all[block], g_all[block], lse_all[block], delta_all[block]
                )
                dv_all[n] += dv
                dk_all[n] += dk
                dqt[block] += dq

            return carry

        lax.fori_loop(0, 8, step, 0)

    for m, ref in enumerate((dq0, dq1, dq2, dq3)):
        for zh in range(2):
            block, at = zh * 2 + m // 2, 256 * (m % 2)
            ref[256 * zh : 256 * zh + 256, :] = (dqt[block, :, at : at + 256].T * SCALE).astype(ref.dtype)
    for d, ref in enumerate((dkv0, dkv1, dkv2, dkv3)):
        for zh in range(2):
            n = 2 * d + zh
            ref[128 * zh : 128 * zh + 128, :HD] = (dk_all[n] * SCALE).astype(ref.dtype)
            ref[128 * zh : 128 * zh + 128, HD:] = dv_all[n].astype(ref.dtype)


def unsort_kernel(dq0, dq1, dq2, dq3, dkv0, dkv1, dkv2, dkv3, dkvn_ref, copy_ref, out_ref):
    dq = dq0[...] + dq1[...].astype(F32) + dq2[...].astype(F32) + dq3[...].astype(F32)
    dkv = dkv0[...] + dkv1[...].astype(F32) + dkv2[...].astype(F32) + dkv3[...].astype(F32)
    dq, dkv = dq.astype(BF16), dkv.astype(BF16)
    for j in range(RUNS):
        zh, c = divmod(j, 2)
        one_hot = placing(copy_ref, j).T.astype(BF16)
        at = 64 * c
        queries = jnp.concatenate(
            [dq[256 * zh + at : 256 * zh + at + 64], dq[256 * zh + 128 + at : 256 * zh + 192 + at]], axis=0
        )
        keys = jnp.concatenate(
            [dkvn_ref[128 * zh + at : 128 * zh + at + 64, :], dkv[128 * zh + at : 128 * zh + at + 64]], axis=0
        )
        moved = contract(one_hot, jnp.concatenate([queries, keys], axis=1), 1, 0).astype(BF16)
        for z in range(4):
            for i in range(3):
                out_ref[4 * j + z, 32 * i : 32 * i + 32, :] = moved[32 * z : 32 * z + 32, HD * i : HD * (i + 1)]


def unpack_kernel(got_ref, dq_ref, dk_ref, dv_ref):
    rows = dq_ref.shape[0]
    for slot in range(16):
        j, z = divmod(slot, 4)
        h = 4 * z + j
        for i, ref in enumerate((dq_ref, dk_ref, dv_ref)):
            ref[:, h * HD : (h + 1) * HD] = got_ref[slot, i * rows : (i + 1) * rows, :]


def swap(x, axes, mask):
    return lax.ppermute(x, axes, [(i, i ^ mask) for i in range(4)])


def shape(dims, dtype=BF16):
    return jax.ShapeDtypeStruct(dims, dtype)


def per_device(query_in, key_in, value_in, saved_out, grad_out, saved_lse, row_block, row_copy):
    copies = row_copy.reshape(-1, RUN)
    ids = row_block[:: 4 * RUN]
    rows = query_in.shape[0]
    packed = call(
        pack_kernel,
        shape((16, 4 * rows + 16, HD)),
        (query_in, key_in, value_in, saved_out, grad_out, saved_lse.T),
    )
    got = lax.all_to_all(packed, HEAD_AXES, 0, 0, tiled=True)
    qd, kv, kvn = call(
        sort_kernel, (shape((528, 256)), shape((256, 256)), shape((256, 256))), (got, copies)
    )
    qds = [qd] + [None] * 3
    kvs = [kv] + [None] * 3
    for m in (2, 1, 3):
        qds[m] = swap(qd, QUERY_AXES, m)
        kvs[m] = swap(kv, KEY_AXES, m)
    outs = (
        [shape((512, HD), F32)] + [shape((512, HD))] * 3
        + [shape((256, 256), F32)] + [shape((256, 256))] * 3 + [shape((256, 256))]
    )
    scratch = (
        pltpu.VMEM((4, 512, HD), BF16), pltpu.VMEM((4, 512, HD), BF16),
        pltpu.VMEM((4, 1, 512), F32), pltpu.VMEM((4, 1, 512), F32),
        pltpu.VMEM((8, 128, HD), BF16), pltpu.VMEM((8, HD, 128), BF16), pltpu.VMEM((8, 128, HD), BF16),
        pltpu.VMEM((4, HD, 512), F32), pltpu.VMEM((8, 128, HD), F32), pltpu.VMEM((8, 128, HD), F32),
    )
    results = call(attend_kernel, outs, (ids, *qds, *kvs, kvn), smem=(0,), scratch=scratch)
    dqs, dkvs, dkvn = list(results[:4]), list(results[4:8]), results[8]
    for m in (2, 1, 3):
        dqs[m] = swap(dqs[m], QUERY_AXES, m)
        dkvs[m] = swap(dkvs[m], KEY_AXES, m)
    back = call(unsort_kernel, shape((16, 3 * rows, HD)), (*dqs, *dkvs, dkvn, copies))
    back = lax.all_to_all(back, HEAD_AXES, 0, 0, tiled=True)
    return call(unpack_kernel, (shape((rows, 16 * HD)),) * 3, (back,))


def solution(mesh):
    fine = Mesh(mesh.devices.reshape(SIZES), AXES)
    whole = P(AXES, None)
    return jax.shard_map(
        per_device,
        mesh=fine,
        in_specs=(whole, whole, whole, whole, whole, P(AXES[:5], AXES[5]), P(), P()),
        out_specs=(whole, whole, whole),
        check_vma=False,
    )
```

time: 712 us -> 98.3 us (0.14)
  the two profiles are of different devices: /device:TPU:10 before, /device:TPU:1 now
where the time goes in v1:
time: 98.3 us; the launch traced here: 97.2 us
  blocking collectives  46.5 us (47%)
  starting transfers between devices  18.8 us (19%)
  waiting for transfers between devices  13.9 us (14%)
  Pallas kernels  11.3 us (11%)
  local copies, waits for them, and re-layouts  6.05 us (6%)
    all_to_all x1, blocking collectives, per_device(): got = lax.all_to_all(packed, HEAD_AXES, 0, 0, tiled=True)  28.7 us
    ppermute x12, starting transfers between devices, swap(): return lax.ppermute(x, axes, [(i, i ^ mask) for i in range(4)])  18.8 us
    all_to_all x1, blocking collectives, per_device(): back = lax.all_to_all(back, HEAD_AXES, 0, 0, tiled=True)  17.8 us
    ppermute x12, waiting for transfers between devices, swap(): return lax.ppermute(x, axes, [(i, i ^ mask) for i in range(4)])  13.9 us
    pallas_call x5, Pallas kernels, call(): pl.pallas_call(body, out_shape=out_shape, in_specs=[SMEM if i in smem els...  11.3 us
    unnamed x14, local copies, waits for them, and re-layouts  5.2 us
  transfers between devices with their start and end apart: 12, of which 4 were waited for; matrix products, arithmetic and copies ran while one was open for 1% of the time, Pallas kernels for 0%

profile of v1, /device:TPU:1, one launch (start us, length us, event | category | flops | bytes accessed | tf_op | source)
XLA Modules:
  0.0 97.2 jit_solution(15629238221150376576)
XLA Ops:
  0.6 0.0 copy-start.1
  0.6 0.9 copy-done.1
  1.5 0.0 copy-start.2
  1.5 0.9 copy-done.2
  2.4 0.0 copy-start.3
  2.4 0.9 copy-done.3
  3.3 0.0 copy-start.4
  3.3 0.9 copy-done.4
  4.3 0.0 copy-start.5
  4.3 0.9 copy-done.5
  5.2 0.0 copy-start.6
  5.2 0.7 copy-done.6
  5.8 0.2 shard_map.103
  6.1 0.0 copy-start
  6.1 28.7 %all_to_all.10.got_ref = bf16[16,144,128]{2,1,0:T(8,128)(2,1)S(1)} all-to-all(bf16[16,144,128]{2,1,0:T(8,128)(2,1)S(1)} %shard_map.103), channel_id=1, replica_groups=mesh['y'=4,'zh'=2,'xh'=2,'xl'=2,'c'=2,'zl'=4] {'zh','c','zl'}, dimensions={0} | all-to-all | bytes 1179648 | tf_op jit(solution)/shard_map/all_to_all | solution.py:261
  34.8 0.0 copy-done
  34.8 0.9 shard_map.104
  35.6 2.5 %collective-permute-start.2 = (bf16[528,256]{1,0:T(8,128)(2,1)S(1)}, bf16[528,256]{1,0:T(8,128)(2,1)S(1)}, u32[]{:S(2)}, u32[]{:S(2)}) collective-permute-start(bf16[528,256]{1,0:T(8,128)(2,1)S(1)} %get-tuple-element.15.qd0), channel_id=1, source_target_pairs={{0,24},{8,16},{16,8},{24,0},{1,25},{9,17},{17,9},{25,1},{2,26},{10... | collective-permute-start | bytes 811016 | tf_op jit(solution)/shard_map/ppermute | solution.py:245
  38.1 0.5 collective-permute-start.1
  38.7 0.2 collective-permute-start
  38.9 2.7 %collective-permute-start.5 = (bf16[256,256]{1,0:T(8,128)(2,1)S(1)}, bf16[256,256]{1,0:T(8,128)(2,1)S(1)}, u32[]{:S(2)}, u32[]{:S(2)}) collective-permute-start(bf16[256,256]{1,0:T(8,128)(2,1)S(1)} %get-tuple-element.16.kv0), channel_id=1, source_target_pairs={{0,192},{64,128},{128,64},{192,0},{1,193},{65,129},{129,65},{193,1... | collective-permute-start | bytes 393224 | tf_op jit(solution)/shard_map/ppermute | solution.py:245
  41.6 0.3 collective-permute-start.4
  42.0 5.3 %collective-permute-done.5.kv3 = bf16[256,256]{1,0:T(8,128)(2,1)S(1)} collective-permute-done((bf16[256,256]{1,0:T(8,128)(2,1)S(1)}, bf16[256,256]{1,0:T(8,128)(2,1)S(1)}, u32[]{:S(2)}, u32[]{:S(2)}) %collective-permute-start.5) | collective-permute-done | bytes 131104 | tf_op jit(solution)/shard_map/ppermute | solution.py:245
  47.3 0.0 collective-permute-start.3
  47.3 0.8 slice.3.ids_ref
  48.2 0.0 collective-permute-done.4.kv2
  48.2 3.3 %collective-permute-done.3.kv1 = bf16[256,256]{1,0:T(8,128)(2,1)S(1)} collective-permute-done((bf16[256,256]{1,0:T(8,128)(2,1)S(1)}, bf16[256,256]{1,0:T(8,128)(2,1)S(1)}, u32[]{:S(2)}, u32[]{:S(2)}) %collective-permute-start.3) | collective-permute-done | bytes 131104 | tf_op jit(solution)/shard_map/ppermute | solution.py:245
  51.5 0.0 collective-permute-done.2.qd3
  51.5 0.0 collective-permute-done.1.qd2
  51.5 0.0 collective-permute-done.qd1
  51.5 8.3 %shard_map.105 = (f32[512,128]{1,0:T(8,128)S(1)}, bf16[512,128]{1,0:T(8,128)(2,1)S(1)}, bf16[512,128]{1,0:T(8,128)(2,1)S(1)}, bf16[512,128]{1,0:T(8,128)(2,1)S(1...) custom-call(s32[16]{0:T(128)S(1)} %slice.3.ids_ref, ...), custom_call_target="tpu_custom_call" | custom-call | tf_op jit(solution)/shard_map/pallas_call | solution.py:42
  59.8 1.3 %collective-permute-start.6 = (bf16[512,128]{1,0:T(8,128)(2,1)S(1)}, bf16[512,128]{1,0:T(8,128)(2,1)S(1)}, u32[]{:S(2)}, u32[]{:S(2)}) collective-permute-start(bf16[512,128]{1,0:T(8,128)(2,1)S(1)} %get-tuple-element.19), channel_id=1, source_target_pairs={{0,8},{8,0},{16,24},{24,16},{1,9},{9,1},{17,25},{25,17},{2,10},{10... | collective-permute-start | bytes 393224 | tf_op jit(solution)/shard_map/ppermute | solution.py:245
  61.1 1.7 %collective-permute-start.7 = (bf16[512,128]{1,0:T(8,128)(2,1)S(1)}, bf16[512,128]{1,0:T(8,128)(2,1)S(1)}, u32[]{:S(2)}, u32[]{:S(2)}) collective-permute-start(bf16[512,128]{1,0:T(8,128)(2,1)S(1)} %get-tuple-element.20), channel_id=1, source_target_pairs={{0,16},{8,24},{16,0},{24,8},{1,17},{9,25},{17,1},{25,9},{2,18},{10... | collective-permute-start | bytes 393224 | tf_op jit(solution)/shard_map/ppermute | solution.py:245
  62.8 1.0 %collective-permute-start.8 = (bf16[512,128]{1,0:T(8,128)(2,1)S(1)}, bf16[512,128]{1,0:T(8,128)(2,1)S(1)}, u32[]{:S(2)}, u32[]{:S(2)}) collective-permute-start(bf16[512,128]{1,0:T(8,128)(2,1)S(1)} %get-tuple-element.21), channel_id=1, source_target_pairs={{0,24},{8,16},{16,8},{24,0},{1,25},{9,17},{17,9},{25,1},{2,26},{10... | collective-permute-start | bytes 393224 | tf_op jit(solution)/shard_map/ppermute | solution.py:245
  63.7 0.0 collective-permute-start.9
  63.8 8.2 %collective-permute-start.10 = (bf16[256,256]{1,0:T(8,128)(2,1)S(1)}, bf16[256,256]{1,0:T(8,128)(2,1)S(1)}, u32[]{:S(2)}, u32[]{:S(2)}) collective-permute-start(bf16[256,256]{1,0:T(8,128)(2,1)S(1)} %get-tuple-element.24), channel_id=1, source_target_pairs={{0,128},{64,192},{128,0},{192,64},{1,129},{65,193},{129,1},{193,65... | collective-permute-start | bytes 393224 | tf_op jit(solution)/shard_map/ppermute | solution.py:245
  72.0 0.0 collective-permute-done.6.dq1
  72.0 0.3 collective-permute-start.11
  72.3 0.0 collective-permute-done.7.dq2
  72.3 0.0 collective-permute-done.8.dq3
  72.3 0.0 collective-permute-done.9.dkv1
  72.3 3.7 %collective-permute-done.10.dkv2 = bf16[256,256]{1,0:T(8,128)(2,1)S(1)} collective-permute-done((bf16[256,256]{1,0:T(8,128)(2,1)S(1)}, bf16[256,256]{1,0:T(8,128)(2,1)S(1)}, u32[]{:S(2)}, u32[]{:S(2)}) %collective-permute-start.10) | collective-permute-done | bytes 131104 | tf_op jit(solution)/shard_map/ppermute | solution.py:245
  76.0 1.5 %collective-permute-done.11.dkv3 = bf16[256,256]{1,0:T(8,128)(2,1)S(1)} collective-permute-done((bf16[256,256]{1,0:T(8,128)(2,1)S(1)}, bf16[256,256]{1,0:T(8,128)(2,1)S(1)}, u32[]{:S(2)}, u32[]{:S(2)}) %collective-permute-start.11) | collective-permute-done | bytes 131104 | tf_op jit(solution)/shard_map/ppermute | solution.py:245
  77.5 1.1 %shard_map.106 = bf16[16,96,128]{2,1,0:T(8,128)(2,1)S(1)} custom-call(f32[512,128]{1,0:T(8,128)S(1)} %get-tuple-element.18.dq0, bf16[512,128]{1,0:T(8,128)(2,1)S(1)} %collective-permute-done.6.dq1, bf16[512,128]{1,0:T(8,128)(2,1)S(1)} %collective-permute-done.7.dq2, bf16[512,128]{1,0:T(8,128)(2,1)S(1)} %collective-permute-done.8.dq3, ...), custom_call_target="tpu_custom_call" | custom-call | tf_op jit(solution)/shard_map/pallas_call | solution.py:42
  78.6 17.8 %all_to_all.11.got_ref = bf16[16,96,128]{2,1,0:T(8,128)(2,1)S(1)} all-to-all(bf16[16,96,128]{2,1,0:T(8,128)(2,1)S(1)} %shard_map.106), channel_id=1, replica_groups=mesh['y'=4,'zh'=2,'xh'=2,'xl'=2,'c'=2,'zl'=4] {'zh','c','zl'}, dimensions={0} | all-to-all | bytes 786432 | tf_op jit(solution)/shard_map/all_to_all | solution.py:286
  96.4 0.8 shard_map.107
Async XLA Ops:
  0.6 0.9 copy-start.1
  1.5 0.9 copy-start.2
  2.4 0.9 copy-start.3
  3.3 0.9 copy-start.4
  4.3 0.9 copy-start.5
  5.2 0.7 copy-start.6
  6.1 28.7 %copy-start = (s32[8192]{0:T(1024)S(1)}, s32[8192]{0:T(1024)}, u32[]{:S(2)}) copy-start(s32[8192]{0:T(1024)} %param.15) | copy-start | bytes 98308
  35.6 15.8 %collective-permute-start.2 = (bf16[528,256]{1,0:T(8,128)(2,1)S(1)}, bf16[528,256]{1,0:T(8,128)(2,1)S(1)}, u32[]{:S(2)}, u32[]{:S(2)}) collective-permute-start(bf16[528,256]{1,0:T(8,128)(2,1)S(1)} %get-tuple-element.15.qd0), channel_id=1, source_target_pairs={{0,24},{8,16},{16,8},{24,0},{1,25},{9,17},{17,9},{25,1},{2,26},{10... | collective-permute-start | bytes 811016 | tf_op jit(solution)/shard_map/ppermute | solution.py:245
  38.1 13.3 %collective-permute-start.1 = (bf16[528,256]{1,0:T(8,128)(2,1)S(1)}, bf16[528,256]{1,0:T(8,128)(2,1)S(1)}, u32[]{:S(2)}, u32[]{:S(2)}) collective-permute-start(bf16[528,256]{1,0:T(8,128)(2,1)S(1)} %get-tuple-element.15.qd0), channel_id=1, source_target_pairs={{0,16},{8,24},{16,0},{24,8},{1,17},{9,25},{17,1},{25,9},{2,18},{10... | collective-permute-start | bytes 811016 | tf_op jit(solution)/shard_map/ppermute | solution.py:245
  38.7 12.8 %collective-permute-start = (bf16[528,256]{1,0:T(8,128)(2,1)S(1)}, bf16[528,256]{1,0:T(8,128)(2,1)S(1)}, u32[]{:S(2)}, u32[]{:S(2)}) collective-permute-start(bf16[528,256]{1,0:T(8,128)(2,1)S(1)} %get-tuple-element.15.qd0), channel_id=1, source_target_pairs={{0,8},{8,0},{16,24},{24,16},{1,9},{9,1},{17,25},{25,17},{2,10},{10... | collective-permute-start | bytes 811016 | tf_op jit(solution)/shard_map/ppermute | solution.py:245
  38.9 8.4 %collective-permute-start.5 = (bf16[256,256]{1,0:T(8,128)(2,1)S(1)}, bf16[256,256]{1,0:T(8,128)(2,1)S(1)}, u32[]{:S(2)}, u32[]{:S(2)}) collective-permute-start(bf16[256,256]{1,0:T(8,128)(2,1)S(1)} %get-tuple-element.16.kv0), channel_id=1, source_target_pairs={{0,192},{64,128},{128,64},{192,0},{1,193},{65,129},{129,65},{193,1... | collective-permute-start | bytes 393224 | tf_op jit(solution)/shard_map/ppermute | solution.py:245
  41.6 6.5 %collective-permute-start.4 = (bf16[256,256]{1,0:T(8,128)(2,1)S(1)}, bf16[256,256]{1,0:T(8,128)(2,1)S(1)}, u32[]{:S(2)}, u32[]{:S(2)}) collective-permute-start(bf16[256,256]{1,0:T(8,128)(2,1)S(1)} %get-tuple-element.16.kv0), channel_id=1, source_target_pairs={{0,128},{64,192},{128,0},{192,64},{1,129},{65,193},{129,1},{193,65... | collective-permute-start | bytes 393224 | tf_op jit(solution)/shard_map/ppermute | solution.py:245
  47.3 4.2 %collective-permute-start.3 = (bf16[256,256]{1,0:T(8,128)(2,1)S(1)}, bf16[256,256]{1,0:T(8,128)(2,1)S(1)}, u32[]{:S(2)}, u32[]{:S(2)}) collective-permute-start(bf16[256,256]{1,0:T(8,128)(2,1)S(1)} %get-tuple-element.16.kv0), channel_id=1, source_target_pairs={{0,64},{64,0},{128,192},{192,128},{1,65},{65,1},{129,193},{193,129... | collective-permute-start | bytes 393224 | tf_op jit(solution)/shard_map/ppermute | solution.py:245
  59.8 12.2 %collective-permute-start.6 = (bf16[512,128]{1,0:T(8,128)(2,1)S(1)}, bf16[512,128]{1,0:T(8,128)(2,1)S(1)}, u32[]{:S(2)}, u32[]{:S(2)}) collective-permute-start(bf16[512,128]{1,0:T(8,128)(2,1)S(1)} %get-tuple-element.19), channel_id=1, source_target_pairs={{0,8},{8,0},{16,24},{24,16},{1,9},{9,1},{17,25},{25,17},{2,10},{10... | collective-permute-start | bytes 393224 | tf_op jit(solution)/shard_map/ppermute | solution.py:245
  61.1 11.2 %collective-permute-start.7 = (bf16[512,128]{1,0:T(8,128)(2,1)S(1)}, bf16[512,128]{1,0:T(8,128)(2,1)S(1)}, u32[]{:S(2)}, u32[]{:S(2)}) collective-permute-start(bf16[512,128]{1,0:T(8,128)(2,1)S(1)} %get-tuple-element.20), channel_id=1, source_target_pairs={{0,16},{8,24},{16,0},{24,8},{1,17},{9,25},{17,1},{25,9},{2,18},{10... | collective-permute-start | bytes 393224 | tf_op jit(solution)/shard_map/ppermute | solution.py:245
  62.8 9.5 %collective-permute-start.8 = (bf16[512,128]{1,0:T(8,128)(2,1)S(1)}, bf16[512,128]{1,0:T(8,128)(2,1)S(1)}, u32[]{:S(2)}, u32[]{:S(2)}) collective-permute-start(bf16[512,128]{1,0:T(8,128)(2,1)S(1)} %get-tuple-element.21), channel_id=1, source_target_pairs={{0,24},{8,16},{16,8},{24,0},{1,25},{9,17},{17,9},{25,1},{2,26},{10... | collective-permute-start | bytes 393224 | tf_op jit(solution)/shard_map/ppermute | solution.py:245
  63.7 8.5 %collective-permute-start.9 = (bf16[256,256]{1,0:T(8,128)(2,1)S(1)}, bf16[256,256]{1,0:T(8,128)(2,1)S(1)}, u32[]{:S(2)}, u32[]{:S(2)}) collective-permute-start(bf16[256,256]{1,0:T(8,128)(2,1)S(1)} %get-tuple-element.23), channel_id=1, source_target_pairs={{0,64},{64,0},{128,192},{192,128},{1,65},{65,1},{129,193},{193,129... | collective-permute-start | bytes 393224 | tf_op jit(solution)/shard_map/ppermute | solution.py:245
  63.8 12.3 %collective-permute-start.10 = (bf16[256,256]{1,0:T(8,128)(2,1)S(1)}, bf16[256,256]{1,0:T(8,128)(2,1)S(1)}, u32[]{:S(2)}, u32[]{:S(2)}) collective-permute-start(bf16[256,256]{1,0:T(8,128)(2,1)S(1)} %get-tuple-element.24), channel_id=1, source_target_pairs={{0,128},{64,192},{128,0},{192,64},{1,129},{65,193},{129,1},{193,65... | collective-permute-start | bytes 393224 | tf_op jit(solution)/shard_map/ppermute | solution.py:245
  72.0 5.5 %collective-permute-start.11 = (bf16[256,256]{1,0:T(8,128)(2,1)S(1)}, bf16[256,256]{1,0:T(8,128)(2,1)S(1)}, u32[]{:S(2)}, u32[]{:S(2)}) collective-permute-start(bf16[256,256]{1,0:T(8,128)(2,1)S(1)} %get-tuple-element.25), channel_id=1, source_target_pairs={{0,192},{64,128},{128,64},{192,0},{1,193},{65,129},{129,65},{193,1... | collective-permute-start | bytes 393224 | tf_op jit(solution)/shard_map/ppermute | solution.py:245
